TPU v7x, 32 devices: a whole 2x2x4 slice. The times are simulated.
32 devices in a mesh: dp: 16 (over z, y, core), mp: 2 (over x).
Axes of the slice: x: 2, y: 2, z: 4, core: 2. Of those that a mesh axis runs over, the one named last changes fastest.
Arguments:
- hidden_states: bfloat16 [8192, 2560], P('dp'), may hold values from -16 to 16
- head_weight: bfloat16 [2560, 1024], P(None, 'mp'), may hold values from -1 to 1
- agent_bias: float32 [8, 1024], P(None, 'mp'), may hold values from -6 to 6
- agent_ids: int32 [8192], P('dp'), may hold values from 0 to 7
- actions: int32 [8192], P('dp'), may hold values from 0 to 1023
- rewards: float32 [8192], P('dp'), may hold values from -18 to 18
- values: float32 [8192], P('dp'), may hold values from -6 to 6
- episode_start: int32 [8192], P('dp'), may hold values 0 or 1
- prior_ratio: float32 [8192], P('dp'), may hold values from 0.5 to 2
- sample_rows: int32 [32768], P('dp'), may hold values from 0 to 8191, as said below
Outputs:
- natural_step: float32 [2560, 1024], P(None, 'mp')
Inputs may be any that keep to these rules, and one draw needn't show every extreme that they name: `sample_rows`: each aligned block of 2048 entries names rows of the matching block of 512 rows of hidden_states; a row may be named more than once.
All inputs are finite; a program needn't handle non-finite values. No bound on the sum of `episode_start` on one device may be relied on, other than what follows from the above.
Results may differ from a plain program's by a relative error of at most 0.003.
Values may be sent and summed in bfloat16 or wider, within the bound.
No kernel may reach another device: no remote copies, remote signals or barrier semaphores. Data moves between devices by JAX's collectives and lax.ppermute only.
A program may use at most 128 MiB of HBM per device.

v0:
```python
import jax
import jax.numpy as jnp
from jax import lax
from jax.sharding import PartitionSpec as P

D = 2560
A = 1024
AGENTS = 8
SEQ_LEN = 64
ITERS = 2


GAMMA = 0.99
TRACE_DECAY = 0.95
DAMPING = 0.001
RADIUS_SHARE = 0.001


def advantages(rewards, values, episode_start):
    reward_rows = rewards.reshape(-1, SEQ_LEN)
    value_rows = values.reshape(-1, SEQ_LEN)
    start_rows = episode_start.reshape(-1, SEQ_LEN)
    episode_end = jnp.concatenate([start_rows[:, 1:], jnp.ones_like(start_rows[:, :1])], axis=1)
    continues = (1 - episode_end).astype(jnp.float32)
    value_next = jnp.concatenate([value_rows[:, 1:], jnp.zeros_like(value_rows[:, :1])], axis=1)
    temporal = reward_rows + GAMMA * continues * value_next - value_rows

    def backward(running, inputs):
        error, keeps = inputs
        updated = error + GAMMA * TRACE_DECAY * keeps * running
        return (updated, updated)

    final_state, advantage = lax.scan(
        backward,
        jnp.zeros((reward_rows.shape[0],), jnp.float32),
        (temporal.T, continues.T),
        reverse=True,
    )
    return advantage.T.reshape(-1)


def transpose_product(left, right):
    return lax.dot_general(
        left, right, (((0,), (0,)), ((), ())), preferred_element_type=jnp.float32
    )


def per_device(
    hidden_states,
    head_weight,
    agent_bias,
    agent_ids,
    actions,
    rewards,
    values,
    episode_start,
    prior_ratio,
    sample_rows,
):
    width_data = lax.axis_size("dp")
    local_actions = head_weight.shape[1]
    row_count = hidden_states.shape[0] * width_data
    samples_all = sample_rows.shape[0] * width_data
    advantage = advantages(rewards, values, episode_start)
    adv_total = lax.psum(jnp.sum(advantage), "dp")
    adv_mean = adv_total / row_count
    weight = prior_ratio * (advantage - adv_mean) / row_count
    agent_table = (agent_ids[:, None] == jnp.arange(AGENTS, dtype=jnp.int32)[None, :]).astype(
        jnp.float32
    )
    logits = jnp.dot(hidden_states, head_weight, preferred_element_type=jnp.float32)
    logits = logits + jnp.dot(agent_table, agent_bias, precision=lax.Precision.HIGHEST)
    local_peak = jnp.max(logits, axis=1)
    row_peak = lax.pmax(local_peak, "mp")
    exponent = jnp.exp(logits - row_peak[:, None])
    denominator = lax.psum(jnp.sum(exponent, axis=1), "mp")
    probs = exponent / denominator[:, None]
    action_base = lax.axis_index("mp") * local_actions
    picked = (
        actions[:, None] - action_base == jnp.arange(local_actions, dtype=jnp.int32)[None, :]
    ).astype(jnp.float32)
    logit_grad = (weight[:, None] * (picked - probs)).astype(jnp.bfloat16)
    local_rows = sample_rows - lax.axis_index("dp") * hidden_states.shape[0]
    sampled = jnp.take(hidden_states, local_rows, axis=0)
    sprobs = jnp.take(probs, local_rows, axis=0)
    grad = lax.psum(transpose_product(hidden_states, logit_grad), "dp")

    def global_dots(terms):
        return lax.psum((terms[0],), "mp")

    solution = jnp.zeros_like(grad)
    resid = grad
    direction = grad
    (resid_sq,) = global_dots((jnp.sum(resid * resid),))
    quad = jnp.float32(0.0)
    for iteration in range(ITERS):
        fisher_lifted = jnp.dot(
            sampled, direction.astype(jnp.bfloat16), preferred_element_type=jnp.float32
        )
        centre = lax.psum(jnp.sum(sprobs * fisher_lifted, axis=1), "mp")
        weighted = (sprobs * (fisher_lifted - centre[:, None])).astype(jnp.bfloat16)
        summed = lax.psum(transpose_product(sampled, weighted), "dp")
        fisher_image = summed / samples_all + DAMPING * direction
        (curvature,) = global_dots((jnp.sum(direction * fisher_image),))
        step_size = resid_sq / curvature
        solution = solution + step_size * direction
        resid = resid - step_size * fisher_image
        if iteration + 1 < ITERS:
            (resid_next,) = global_dots((jnp.sum(resid * resid),))
        quad = quad + step_size * step_size * curvature
        if iteration + 1 < ITERS:
            direction = resid + resid_next / resid_sq * direction
            resid_sq = resid_next
    natural_step = solution * jnp.sqrt(D * A * RADIUS_SHARE / quad)
    return natural_step


def solution(mesh):
    placed = (
        P("dp", None),
        P(None, "mp"),
        P(None, "mp"),
        P("dp"),
        P("dp"),
        P("dp"),
        P("dp"),
        P("dp"),
        P("dp"),
        P("dp"),
    )
    return jax.shard_map(
        per_device, mesh=mesh, in_specs=placed, out_specs=P(None, "mp"), check_vma=False
    )
```

profile of v0, /device:TPU:0, one launch (start us, length us, event | category | flops | bytes accessed | tf_op | source)
XLA Modules:
  0.0 571.6 jit_solution(5045793302212610912)
XLA Ops:
  6.5 0.9 reshape.29
  7.5 0.8 reshape.27
  9.3 4.8 while.17
  14.8 35.5 %psum.77 = f32[]{:T(128)} all-reduce(f32[]{:T(128)} %reduce_sum.72), channel_id=1, replica_groups=mesh['dp'=16,'mp'=2] {'dp'}, use_global_device_ids=true, to_apply=%region_3.4 | all-reduce | flops 1 | bytes 8 | tf_op jit(solution)/shard_map/psum | solution.py:65
  51.1 3.3 fusion.23
  54.5 1.7 fusion.22
  56.2 4.9 pmax.7
  61.1 1.4 fusion.15
  62.5 4.9 psum.78
  67.5 2.4 fusion.14
  69.9 5.1 convolution_bitcast_fusion
  75.0 2.5 copy.19
  77.6 11.5 %gather_fusion = bf16[2048,2560]{1,0:T(8,128)(2,1)} fusion(bf16[512,2560]{1,0:T(8,128)(2,1)S(1)} %copy-done, s32[2048]{0:T(1024)S(1)} %fusion.19), kind=kCustom, calls=%fused_computation | custom fusion | bytes 20979712 | tf_op jit(solution)/shard_map/jit(_take)/gather | solution.py:84
  89.1 10.8 %gather_fusion.1 = f32[2048,512]{1,0:T(8,128)} fusion(f32[512,512]{1,0:T(8,128)} %copy.19, s32[2048]{0:T(1024)S(1)} %fusion.19), kind=kCustom, calls=%fused_computation.1 | custom fusion | bytes 8396800 | tf_op jit(solution)/shard_map/jit(_take)/gather | solution.py:85
  99.9 5.4 copy.20
  105.3 91.7 %all-reduce.7.cloned.1.call-done = f32[2560,512]{0,1:T(8,128)} async-done(((f32[2560,512]{0,1:T(8,128)}), f32[2560,512]{0,1:T(8,128)}) %all-reduce.7.cloned.1.call-update) | async-done | bytes 5242896 | tf_op jit(solution)/shard_map/psum | solution.py:86
  197.1 12.0 %multiply_reduce_fusion.5 = (f32[2048]{0:T(1024)S(1)}, f32[2048,512]{0,1:T(8,128)}) fusion(f32[2048,512]{0,1:T(8,128)} %copy.20, pred[2048]{0:T(1024)(128)(4,1)S(1)} %compare_and_fusion, f32[2560,512]{0,1:T(8,128)} %all-reduce.7.cloned.1.call-done, bf16[2048,2560]{1,0:T(8,128)(2,1)} %gather_fusion), kind=kOutput, calls=%fused_computation.18 | convolution fusion | flops 5378406400 | bytes 24127488 | tf_op jit(solution)/shard_map/dot_general | solution.py:97
  209.1 5.0 psum.81
  214.1 14.5 %fusion.6 = f32[2560,512]{0,1:T(8,128)} fusion(f32[2048,512]{0,1:T(8,128)} %get-tuple-element.149, f32[2048,512]{0,1:T(8,128)} %copy.20, f32[2048]{0:T(1024)S(1)} %psum.81, pred[2048]{0:T(1024)(128)(4,1)S(1)} %compare_and_fusion, bf16[2048,2560]{1,0:T(8,128)(2,1)} %gather_fusion), kind=kOutput, calls=%fused_computation.23 | convolution fusion | flops 5378146304 | bytes 24127488 | tf_op jit(solution)/shard_map/dot_general | solution.py:43
  228.8 124.4 %all-reduce.9.cloned.1.call-done = f32[2560,512]{0,1:T(8,128)} async-done(((f32[2560,512]{0,1:T(8,128)}), f32[2560,512]{0,1:T(8,128)}) %all-reduce.9.cloned.1.call-update) | async-done | bytes 5242896 | tf_op jit(solution)/shard_map/psum | solution.py:102
  353.2 6.0 %multiply_reduce_fusion.2 = (f32[]{:T(128)}, f32[]{:T(128)}) fusion(f32[2560,512]{0,1:T(8,128)} %all-reduce.7.cloned.1.call-done, f32[2560,512]{0,1:T(8,128)} %all-reduce.9.cloned.1.call-done), kind=kLoop, calls=%fused_computation.11 | loop fusion | flops 9175038 | bytes 10485768 | tf_op jit(solution)/shard_map/reduce_sum | solution.py:104
  359.2 5.6 all-reduce.2
  366.2 6.0 %multiply_reduce_fusion.1 = f32[]{:T(128)} fusion(f32[2560,512]{0,1:T(8,128)} %all-reduce.7.cloned.1.call-done, f32[2560,512]{0,1:T(8,128)} %all-reduce.9.cloned.1.call-done, f32[]{:T(128)S(6)} %div.41), kind=kLoop, calls=%fused_computation.9 | loop fusion | flops 9175039 | bytes 10485768 | tf_op jit(solution)/shard_map/reduce_sum | solution.py:109
  372.2 5.6 psum.84
  379.0 13.9 %multiply_reduce_fusion.4 = (f32[2048]{0:T(1024)S(1)}, f32[2048,512]{0,1:T(8,128)}) fusion(f32[2048,512]{0,1:T(8,128)} %copy.20, pred[2048]{0:T(1024)(128)(4,1)S(1)} %compare_and_fusion, f32[2560,512]{0,1:T(8,128)} %all-reduce.7.cloned.1.call-done, f32[]{:T(128)S(6)} %div.42, f32[2560,512]{0,1:T(8,128)} %all-reduce.9.cloned.1.call-done, f32[]{:T(128)S(6)} %div.41, ...), kind=kOutput, calls=%fused_computation.16 | convolution fusion | flops 5387581440 | bytes 29370376 | tf_op jit(solution)/shard_map/dot_general | solution.py:97
  392.9 5.0 psum.85
  397.9 14.5 %fusion.7 = f32[2560,512]{0,1:T(8,128)} fusion(f32[2048,512]{0,1:T(8,128)} %get-tuple-element.151, f32[2048,512]{0,1:T(8,128)} %copy.20, f32[2048]{0:T(1024)S(1)} %psum.85, pred[2048]{0:T(1024)(128)(4,1)S(1)} %compare_and_fusion, bf16[2048,2560]{1,0:T(8,128)(2,1)} %gather_fusion), kind=kOutput, calls=%fused_computation.24 | convolution fusion | flops 5378146304 | bytes 24127488 | tf_op jit(solution)/shard_map/dot_general | solution.py:43
  412.4 124.6 %all-reduce.11.cloned.1.call-done = f32[2560,512]{0,1:T(8,128)} async-done(((f32[2560,512]{0,1:T(8,128)}), f32[2560,512]{0,1:T(8,128)}) %all-reduce.11.cloned.1.call-update) | async-done | bytes 5242896 | tf_op jit(solution)/shard_map/psum | solution.py:102
  537.1 7.2 %multiply_reduce_fusion = f32[]{:T(128)} fusion(f32[2560,512]{0,1:T(8,128)} %all-reduce.11.cloned.1.call-done, f32[2560,512]{0,1:T(8,128)} %all-reduce.7.cloned.1.call-done, f32[]{:T(128)S(6)} %div.42, f32[2560,512]{0,1:T(8,128)} %all-reduce.9.cloned.1.call-done, f32[]{:T(128)S(6)} %div.41), kind=kLoop, calls=%fused_computation.7 | loop fusion | flops 15728639 | bytes 15728652 | tf_op jit(solution)/shard_map/reduce_sum | solution.py:104
  544.9 5.6 psum.87
  552.6 6.7 %add_multiply_fusion = f32[2560,512]{0,1:T(8,128)} fusion(f32[2560,512]{0,1:T(8,128)} %all-reduce.7.cloned.1.call-done, f32[]{:T(128)S(6)} %sqrt.3, f32[]{:T(128)S(6)} %div.44, f32[]{:T(128)S(6)} %div.41, f32[]{:T(128)S(6)} %div.42, f32[2560,512]{0,1:T(8,128)} %all-reduce.9.cloned.1.call-done), kind=kLoop, calls=%fused_computation.6 | loop fusion | flops 14417920 | bytes 15728656 | tf_op jit(solution)/shard_map/mul | solution.py:114
  559.2 5.9 %copy.23 = f32[2560,512]{1,0:T(8,128)} copy(f32[2560,512]{0,1:T(8,128)} %add_multiply_fusion) | data formatting | bytes 10485760 | tf_op jit(solution)/shard_map/mul | solution.py:114
  (165 shorter events, 6.0 us)
Async XLA Ops:
  6.5 44.6 %copy-start = (bf16[512,2560]{1,0:T(8,128)(2,1)S(1)}, bf16[512,2560]{1,0:T(8,128)(2,1)}, u32[]{:S(2)}) copy-start(bf16[512,2560]{1,0:T(8,128)(2,1)} %param.12) | copy-start | bytes 7864324
  6.5 190.5 %all-reduce.7.cloned.1.call-start = ((), (), s32[]{:S(2)}) async-start(), calls=%async_computation | async-start | bytes 10485760 | tf_op jit(solution)/shard_map/psum | solution.py:86
  51.1 3.4 copy-start.3
  51.1 3.4 copy-start.6
  54.5 15.4 %copy-start.5 = (s32[512]{0:T(512)S(1)}, s32[512]{0:T(512)}, u32[]{:S(2)}) copy-start(s32[512]{0:T(512)} %param.16) | copy-start | bytes 6148
  54.5 15.3 %copy-start.4 = (f32[512]{0:T(512)S(1)}, f32[512]{0:T(512)}, u32[]{:S(2)}) copy-start(f32[512]{0:T(512)} %param.20) | copy-start | bytes 6148
  75.0 2.6 copy-start.2
  75.0 278.2 %all-reduce.9.cloned.1.call-start = ((), (), s32[]{:S(2)}) async-start(), calls=%async_computation.1 | async-start | bytes 10485760 | tf_op jit(solution)/shard_map/psum | solution.py:102
  228.6 308.5 %all-reduce.11.cloned.1.call-start = ((), (), s32[]{:S(2)}) async-start(), calls=%async_computation.2 | async-start | bytes 10485760 | tf_op jit(solution)/shard_map/psum | solution.py:102
  552.5 12.6 %copy-start.1 = (bf16[512,2560]{1,0:T(8,128)(2,1)S(1)}, bf16[512,2560]{1,0:T(8,128)(2,1)}, u32[]{:S(2)}) copy-start(bf16[512,2560]{1,0:T(8,128)(2,1)} %param.12) | copy-start | bytes 7864324
Sparse Core Ops, SparseCore 0:
  75.1 121.9 all-reduce.6
  228.7 124.4 all-reduce.8
  412.6 124.4 all-reduce.10
where the time goes:
time: 572 us
  waiting for transfers between devices  341 us (60%)
  blocking collectives  72.1 us (13%)
  matrix products  65 us (11%)
  local copies, waits for them, and re-layouts  41.6 us (7%)
  other arithmetic  31.6 us (6%)
  between operations  19.2 us (3%)
    psum x2, waiting for transfers between devices, per_device(): summed = lax.psum(transpose_product(sampled, weighted), 'dp')  249 us
    psum x1, waiting for transfers between devices, per_device(): grad = lax.psum(transpose_product(hidden_states, logit_grad), 'dp')  91.7 us
    psum x1, blocking collectives, per_device(): adv_total = lax.psum(jnp.sum(advantage), 'dp')  35.5 us
    dot_general x3, matrix products, transpose_product(): lax.dot_general(left, right, (((0,), (0,)), ((), ())), preferred_element_...  34.1 us
    dot_general x2, matrix products, per_device(): jnp.dot(sampled, direction.astype(jnp.bfloat16), preferred_element_type=j...  25.9 us
    psum x3, blocking collectives, global_dots(): return lax.psum((terms[0],), 'mp')  16.8 us
    gather x2, local copies, waits for them, and re-layouts, per_device(): sprobs = jnp.take(probs, local_rows, axis=0)  16.2 us
    reduce_sum x2, other arithmetic, per_device(): curvature, = global_dots((jnp.sum(direction * fisher_image),))  13.2 us
  transfers between devices with their start and end apart: 3, of which 3 were waited for; matrix products, arithmetic and copies ran while one was open for 5% of the time, Pallas kernels for 0%

commit v1 on v0

v1 whole, which is shorter than its diff:
```python
import functools

import jax
import jax.numpy as jnp
from jax import lax
from jax.experimental import pallas as pl
from jax.experimental.pallas import tpu as pltpu
from jax.sharding import PartitionSpec as P

SEQ_LEN = 64
GAMMA = 0.99
TRACE_DECAY = 0.95
DAMPING = 0.001
RADIUS_SHARE = 0.001

F32 = jnp.float32
BF16 = jnp.bfloat16
VMEM_LIMIT = 48 * 1024 * 1024
NT = (((1,), (1,)), ((), ()))
TN = (((0,), (0,)), ((), ()))


def call(kernel, name, **kw):
    return pl.pallas_call(
        kernel, name=name, compiler_params=pltpu.CompilerParams(vmem_limit_bytes=VMEM_LIMIT), **kw
    )


def shape(*dims, dtype=F32):
    return jax.ShapeDtypeStruct(dims, dtype)


def total(x):
    return jnp.sum(jnp.sum(x, axis=1, keepdims=True), axis=0, keepdims=True)


def exchanged(x, code, rows, blocks):
    index = lax.broadcasted_iota(jnp.int32, x.shape, 0)
    bit = 1
    while bit < blocks:
        by = rows * bit
        below = lax.bitwise_and(index, by) == 0
        swapped = jnp.where(below, pltpu.roll(x, x.shape[0] - by, 0), pltpu.roll(x, by, 0))
        x = jnp.where(lax.bitwise_and(code, bit) != 0, swapped, x)
        bit *= 2
    return x


def token_kernel(base_ref, rewards_ref, values_ref, starts_ref, samples_ref, adv_ref, sum_ref, count_ref):
    tokens = rewards_ref.shape[1]
    samples = samples_ref.shape[1]

    def shifted(x, by):
        return pltpu.roll(x, tokens - by, 1)

    lane = lax.broadcasted_iota(jnp.int32, (1, tokens), 1)
    last = lax.rem(lane, SEQ_LEN) == SEQ_LEN - 1
    ends = jnp.where(last, 1.0, shifted(starts_ref[...].astype(F32), 1))
    continues = 1.0 - ends
    values = values_ref[...]
    running = rewards_ref[...] + GAMMA * continues * jnp.where(last, 0.0, shifted(values, 1)) - values
    keeps = GAMMA * TRACE_DECAY * continues
    step = 1
    while step < SEQ_LEN:
        running = running + keeps * shifted(running, step)
        keeps = keeps * shifted(keeps, step)
        step *= 2
    adv_ref[...] = running
    sum_ref[...] = jnp.broadcast_to(jnp.sum(running, axis=1, keepdims=True), sum_ref.shape)

    rows = samples_ref[...] - base_ref[0]
    high = (lax.shift_right_arithmetic(rows, 7) == lax.broadcasted_iota(jnp.int32, (8, samples), 0))
    low = (lax.bitwise_and(rows, 127) == lax.broadcasted_iota(jnp.int32, (128, samples), 0))
    table = lax.dot_general(
        high.astype(F32).astype(BF16), low.astype(F32).astype(BF16), NT, preferred_element_type=F32
    )
    for i in range(tokens // 128):
        count_ref[:, i * 128 : (i + 1) * 128] = table[i : i + 1, :]


def token_work(base, rewards, values, starts, samples):
    tokens = rewards.shape[1]
    assert tokens <= 1024 and tokens % 128 == 0
    vmem = pl.BlockSpec(memory_space=pltpu.VMEM)
    return call(
        token_kernel,
        "token_work",
        in_specs=[pl.BlockSpec(memory_space=pltpu.SMEM)] + [vmem] * 4,
        out_shape=(shape(1, tokens), shape(8, 128), shape(1, tokens)),
    )(base, rewards, values, starts, samples)


def logits_kernel(h_ref, w_ref, bias_ref, ids_ref, exp_ref, stats_ref, acc_ref):
    step = pl.program_id(0)
    product = jnp.dot(h_ref[...], w_ref[...], preferred_element_type=F32)

    @pl.when(step == 0)
    def _():
        acc_ref[...] = product

    @pl.when(step > 0)
    def _():
        acc_ref[...] += product

    @pl.when(step == pl.num_programs(0) - 1)
    def _():
        agents = bias_ref.shape[0]
        tokens = ids_ref.shape[1]
        table = (ids_ref[...] == lax.broadcasted_iota(jnp.int32, (agents, tokens), 0)).astype(F32)
        bias = lax.dot_general(
            bias_ref[...], table, TN, precision=lax.Precision.HIGHEST, preferred_element_type=F32
        )
        logits = acc_ref[...].T + bias
        peak = jnp.max(logits, axis=0, keepdims=True)
        exponent = jnp.exp(logits - peak)
        exp_ref[...] = exponent
        stats_ref[0:1, :] = peak
        stats_ref[1:2, :] = jnp.sum(exponent, axis=0, keepdims=True)
        stats_ref[2:8, :] = jnp.zeros((6, tokens), F32)


def logits_work(hidden, weight, bias, ids, tile):
    tokens, width = hidden.shape
    actions = weight.shape[1]
    return call(
        logits_kernel,
        "logits",
        grid=(width // tile,),
        in_specs=[
            pl.BlockSpec((tokens, tile), lambda j: (0, j)),
            pl.BlockSpec((tile, actions), lambda j: (j, 0)),
            pl.BlockSpec(bias.shape, lambda j: (0, 0)),
            pl.BlockSpec(ids.shape, lambda j: (0, 0)),
        ],
        out_specs=(
            pl.BlockSpec((actions, tokens), lambda j: (0, 0)),
            pl.BlockSpec((8, tokens), lambda j: (0, 0)),
        ),
        out_shape=(shape(actions, tokens), shape(8, tokens)),
        scratch_shapes=[pltpu.VMEM((tokens, actions), F32)],
    )(hidden, weight, bias, ids)


def probs_kernel(blocks, row_count, place_ref, exp_ref, stats_ref, *refs):
    *others, adv_ref, sum_ref, prior_ref, actions_ref, own_p, send_p, own_g, send_g = refs
    half = own_p.shape[0]
    rows = half // blocks
    core, code, first = place_ref[0], place_ref[1], place_ref[2]
    own_peak = stats_ref[0:1, :]
    peak = own_peak
    for other in others:
        peak = jnp.maximum(peak, other[0:1, :])
    denominator = stats_ref[1:2, :] * jnp.exp(own_peak - peak)
    for other in others:
        denominator = denominator + other[1:2, :] * jnp.exp(other[0:1, :] - peak)
    scale = jnp.exp(own_peak - peak) / denominator
    weight = prior_ref[...] * (adv_ref[...] - sum_ref[0:1, 0:1] / row_count) / row_count
    action = actions_ref[...] - first

    def hand_out(part, probs, index, p_ref, g_ref):
        picked = (index == action).astype(F32)
        p_ref[part, :] = probs
        g_ref[part, :] = (weight * (picked - probs)).astype(BF16)

    for side, p_ref, g_ref in ((core, own_p, own_g), (1 - core, send_p, send_g)):
        if rows % 16:
            start = pl.multiple_of(side * half, half)
            probs = exp_ref[pl.ds(start, half), :] * scale
            index = start + lax.broadcasted_iota(jnp.int32, probs.shape, 0)
            probs, index = (exchanged(x, code, rows, blocks) for x in (probs, index))
            hand_out(slice(0, half), probs, index, p_ref, g_ref)
            continue
        for k in range(blocks):
            start = pl.multiple_of(side * half + lax.bitwise_xor(code, k) * rows, rows)
            probs = exp_ref[pl.ds(start, rows), :] * scale
            index = start + lax.broadcasted_iota(jnp.int32, probs.shape, 0)
            hand_out(slice(k * rows, (k + 1) * rows), probs, index, p_ref, g_ref)


def probs_work(blocks, row_count, place, exponent, stats, others, adv, adv_sum, prior, actions):
    count, tokens = exponent.shape
    half = count // 2
    vmem = pl.BlockSpec(memory_space=pltpu.VMEM)
    return call(
        functools.partial(probs_kernel, blocks, row_count),
        "probs",
        in_specs=[pl.BlockSpec(memory_space=pltpu.SMEM)] + [vmem] * (6 + len(others)),
        out_shape=(
            shape(half, tokens),
            shape(half, tokens),
            shape(half, tokens, dtype=BF16),
            shape(half, tokens, dtype=BF16),
        ),
    )(place, exponent, stats, *others, adv, adv_sum, prior, actions)


def outer_kernel(pieces, scale, left0, left1, h0, h1, own_ref, *send_refs):
    product = jnp.dot(left0[...], h0[...], preferred_element_type=F32)
    product = product + jnp.dot(left1[...], h1[...], preferred_element_type=F32)
    if scale != 1.0:
        product = product * scale
    rows = product.shape[0] // sum(len(p) for p in pieces)
    for ref, blocks in zip((own_ref, *send_refs), pieces):
        for i, k in enumerate(blocks):
            ref[i * rows : (i + 1) * rows, :] = product[k * rows : (k + 1) * rows].astype(ref.dtype)


def outer_work(pieces, left, hidden, first, columns, tile, scale, wire):
    rows, tokens = left[0].shape
    blocks = sum(len(p) for p in pieces)
    sizes = [len(p) * (rows // blocks) for p in pieces]
    offset = first // tile
    fixed = pl.BlockSpec((rows, tokens), lambda j: (0, 0))
    moving = pl.BlockSpec((tokens, tile), lambda j: (0, j + offset))
    return call(
        functools.partial(outer_kernel, pieces, scale),
        "outer",
        grid=(columns // tile,),
        in_specs=[fixed, fixed, moving, moving],
        out_specs=[pl.BlockSpec((size, tile), lambda j: (0, j)) for size in sizes],
        out_shape=[
            shape(size, columns, dtype=F32 if i == 0 else wire) for i, size in enumerate(sizes)
        ],
    )(*left, *hidden)


def lift_kernel(with_dots, *refs):
    if with_dots:
        v_ref, h0, h1, p0, p1, g_ref, out_ref, centre_ref, dots_ref, acc = refs
    else:
        v_ref, h0, h1, p0, p1, out_ref, centre_ref, acc = refs
    tokens = h0.shape[0]
    step = pl.program_id(0)
    v = v_ref[...]

    @pl.when(step == 0)
    def _():
        acc[...] = jnp.zeros_like(acc)
        if with_dots:
            dots_ref[...] = jnp.zeros_like(dots_ref)

    acc[:, :tokens] += lax.dot_general(v, h0[...], NT, preferred_element_type=F32)
    acc[:, tokens:] += lax.dot_general(v, h1[...], NT, preferred_element_type=F32)
    if with_dots:
        f = v.astype(F32)
        g = g_ref[...].astype(F32)
        row = lax.broadcasted_iota(jnp.int32, dots_ref.shape, 0)
        dots_ref[...] += jnp.where(
            row == 0, total(g * g), jnp.where(row == 1, total(g * f), jnp.where(row == 2, total(f * f), 0.0))
        )

    @pl.when(step == pl.num_programs(0) - 1)
    def _():
        lifted = acc[...]
        out_ref[...] = lifted
        centre_ref[:, :tokens] = jnp.sum(p0[...] * lifted[:, :tokens], axis=0, keepdims=True)
        centre_ref[:, tokens:] = jnp.sum(p1[...] * lifted[:, tokens:], axis=0, keepdims=True)


def lift_work(v, hidden, probs, tile, grad=None):
    rows, width = v.shape
    tokens = hidden[0].shape[0]
    moving = pl.BlockSpec((rows, tile), lambda j: (0, j))
    states = pl.BlockSpec((tokens, tile), lambda j: (0, j))
    fixed = pl.BlockSpec((rows, tokens), lambda j: (0, 0))
    dots = grad is not None
    return call(
        functools.partial(lift_kernel, dots),
        "lift",
        grid=(width // tile,),
        in_specs=[moving, states, states, fixed, fixed] + [moving] * dots,
        out_specs=[
            pl.BlockSpec((rows, 2 * tokens), lambda j: (0, 0)),
            pl.BlockSpec((1, 2 * tokens), lambda j: (0, 0)),
        ]
        + [pl.BlockSpec((8, 128), lambda j: (0, 0))] * dots,
        out_shape=[shape(rows, 2 * tokens), shape(1, 2 * tokens)] + [shape(8, 128)] * dots,
        scratch_shapes=[pltpu.VMEM((rows, 2 * tokens), F32)],
    )(v, *hidden, *probs, *([grad] if dots else []))


def weighted_kernel(lifted, centre, p0, p1, n0, n1, w0, w1, quad_ref):
    tokens = p0.shape[1]
    quad = jnp.zeros((1, 1), F32)
    for i, (p, n, w) in enumerate(((p0, n0, w0), (p1, n1, w1))):
        part = slice(i * tokens, (i + 1) * tokens)
        spread = lifted[:, part] - centre[:, part]
        weighted = n[...] * p[...] * spread
        w[...] = weighted.astype(BF16)
        quad = quad + total(weighted * spread)
    quad_ref[...] = jnp.broadcast_to(quad, quad_ref.shape)


def weighted_work(lifted, centre, probs, counts):
    rows, tokens = probs[0].shape
    return call(
        weighted_kernel,
        "weighted",
        out_shape=(shape(rows, tokens, dtype=BF16), shape(rows, tokens, dtype=BF16), shape(8, 128)),
    )(lifted, centre, *probs, *counts)


def products_kernel(samples, l1, c1, l2, c2, p0, p1, n0, n1, dots_ref, quad_ref, out_ref):
    tokens = p0.shape[1]
    cross = jnp.zeros((1, 1), F32)
    second = jnp.zeros((1, 1), F32)
    for i, (p, n) in enumerate(((p0, n0), (p1, n1))):
        part = slice(i * tokens, (i + 1) * tokens)
        spread = l2[:, part] - c2[:, part]
        weighted = n[...] * p[...] * spread
        cross = cross + total(weighted * (l1[:, part] - c1[:, part]))
        second = second + total(weighted * spread)
    lane = lax.broadcasted_iota(jnp.int32, out_ref.shape, 1)
    terms = (
        dots_ref[0:1, 0:1],
        dots_ref[1:2, 0:1],
        dots_ref[2:3, 0:1],
        quad_ref[0:1, 0:1] / samples,
        cross / samples,
        second / samples,
    )
    out = jnp.zeros(out_ref.shape, F32)
    for i, term in enumerate(terms):
        out = jnp.where(lane == i, term, out)
    out_ref[...] = out


def products_work(samples, copies, l1, c1, l2, c2, probs, counts, dots, quad):
    return call(
        functools.partial(products_kernel, samples),
        "products",
        out_shape=shape(copies, 128),
    )(l1, c1, l2, c2, *probs, *counts, dots, quad)


def final_kernel(blocks, replicas, size, place_ref, sums_ref, g0, g1, f0, f1, out_ref, acc):
    half = g0.shape[0]
    rows = half // blocks
    core, code = place_ref[0], place_ref[1]
    sums = jnp.sum(sums_ref[...], axis=0, keepdims=True)
    gg, gf, ff = (sums[:, i : i + 1] / replicas for i in range(3))
    q11, q12, q22 = (sums[:, i : i + 1] for i in range(3, 6))
    curvature1 = q11 + DAMPING * gg
    step1 = gg / curvature1
    keep = q11 / curvature1
    rr = keep * keep * gg - 2.0 * keep * step1 * gf + step1 * step1 * ff
    beta = rr / gg
    a = keep + beta
    b = -step1
    curvature2 = a * a * q11 + 2.0 * a * b * q12 + b * b * q22
    curvature2 = curvature2 + DAMPING * (a * a * gg + 2.0 * a * b * gf + b * b * ff)
    step2 = rr / curvature2
    quad = step1 * step1 * curvature1 + step2 * step2 * curvature2
    norm = jnp.sqrt(size * RADIUS_SHARE / quad)
    on_g = norm * (step1 + step2 * a)
    on_f = norm * step2 * b
    for side, g, f in ((core, g0, f0), (1 - core, g1, f1)):
        if rows % 16:
            start = pl.multiple_of(side * half, half)
            both = on_g * g[...].astype(F32) + on_f * f[...].astype(F32)
            acc[pl.ds(start, half), :] = exchanged(both, code, rows, blocks)
            continue
        for k in range(blocks):
            start = pl.multiple_of(side * half + lax.bitwise_xor(code, k) * rows, rows)
            part = slice(k * rows, (k + 1) * rows)
            acc[pl.ds(start, rows), :] = on_g * g[part, :].astype(F32) + on_f * f[part, :].astype(F32)
    out_ref[...] = acc[...].T


def final_work(blocks, replicas, size, place, sums, g, f, tile):
    half, width = g[0].shape
    moving = pl.BlockSpec((half, tile), lambda j: (0, j))
    return call(
        functools.partial(final_kernel, blocks, replicas, size),
        "final",
        grid=(width // tile,),
        in_specs=[
            pl.BlockSpec(memory_space=pltpu.SMEM),
            pl.BlockSpec(sums.shape, lambda j: (0, 0)),
        ]
        + [moving] * 4,
        out_specs=pl.BlockSpec((tile, 2 * half), lambda j: (j, 0)),
        out_shape=shape(width, 2 * half),
        scratch_shapes=[pltpu.VMEM((2 * half, tile), F32)],
    )(place, sums, *g, *f)


def per_device(
    hidden_states,
    head_weight,
    agent_bias,
    agent_ids,
    actions,
    rewards,
    values,
    episode_start,
    prior_ratio,
    sample_rows,
):
    data, model = lax.axis_size("dp"), lax.axis_size("mp")
    index, column = lax.axis_index("dp"), lax.axis_index("mp")
    tokens, width = hidden_states.shape
    local_actions = head_weight.shape[1]
    half = local_actions // 2
    row_count = tokens * data
    samples_all = sample_rows.shape[0] * data
    chips = data // 2
    depth = min(4, chips)
    breadth = chips // depth
    core = lax.rem(index, 2)
    chip = index // 2
    code = lax.rem(chip, breadth) * depth + chip // breadth
    block = half // chips
    tile = 512
    columns_a = 3 * tile
    columns_b = width - columns_a

    def swap(x, slow=0, fast=0, other=0):
        mask = ((slow * breadth + fast) << 1) | other
        return lax.ppermute(x, "dp", [(i, i ^ mask) for i in range(data)])

    def swap_model(x, mask):
        return lax.ppermute(x, "mp", [(i, i ^ mask) for i in range(model)])

    def sum_model(x):
        mask = 1
        while mask < model:
            x = x + swap_model(x, mask)
            mask *= 2
        return x

    def sum_group(x):
        y = swap(x, other=1)
        return sum_model(x + jnp.concatenate([y[:, tokens:], y[:, :tokens]], axis=1))

    def reduce_scatter(left, hidden, scale, wire):
        by_slow = [[f * depth + s for f in range(breadth)] for s in range(depth)]
        by_fast = [[f * depth + s for s in range(depth)] for f in range(breadth)]
        own_b, *send_b = outer_work(by_slow, left, hidden, columns_a, columns_b, tile, scale, wire)
        got_b = [swap(x, slow=i + 1) for i, x in enumerate(send_b)]
        own_a, *send_a = outer_work(by_fast, left, hidden, 0, columns_a, tile, scale, wire)
        got_a = [swap(x, fast=i + 1) for i, x in enumerate(send_a)]
        sum_a = sum((x.astype(F32) for x in got_a), own_a)
        got_a = [
            swap(sum_a[s * block : (s + 1) * block].astype(wire), slow=s) for s in range(1, depth)
        ]
        sum_b = sum((x.astype(F32) for x in got_b), own_b)
        got_b = [
            swap(sum_b[f * block : (f + 1) * block].astype(wire), fast=f) for f in range(1, breadth)
        ]
        sum_a = sum((x.astype(F32) for x in got_a), sum_a[:block])
        sum_b = sum((x.astype(F32) for x in got_b), sum_b[:block])
        return sum_a, sum_b

    def all_gather(part_a, part_b):
        a = jnp.concatenate([part_a] + [swap(part_a, slow=s) for s in range(1, depth)])
        b = jnp.concatenate([part_b] + [swap(part_b, fast=f) for f in range(1, breadth)])
        a = jnp.concatenate([a] + [swap(a, fast=f) for f in range(1, breadth)])
        b = jnp.stack([b] + [swap(b, slow=s) for s in range(1, depth)])
        b = b.reshape(depth, breadth, block, columns_b).transpose(1, 0, 2, 3).reshape(half, columns_b)
        return jnp.concatenate([a, b], axis=1)

    row = lambda x: x.reshape(1, -1)
    place = jnp.stack([core, code, column * local_actions]).astype(jnp.int32)
    base = (index * tokens).astype(jnp.int32).reshape(1)

    adv, adv_sum, counts = token_work(
        base, row(rewards), row(values), row(episode_start), row(sample_rows)
    )
    hidden = (hidden_states, swap(hidden_states, other=1))
    mask = 1
    while mask < data:
        adv_sum = adv_sum + lax.ppermute(adv_sum, "dp", [(i, i ^ mask) for i in range(data)])
        mask *= 2
    exponent, stats = logits_work(hidden_states, head_weight, agent_bias, row(agent_ids), tile)
    others = [swap_model(stats, i) for i in range(1, model)]
    own_p, send_p, own_g, send_g = probs_work(
        chips, row_count, place, exponent, stats, others, adv, adv_sum, row(prior_ratio), row(actions)
    )
    left = (own_g, swap(send_g, other=1))
    probs = (own_p, swap(send_p, other=1))
    counts = (counts, swap(counts, other=1))

    grad_a, grad_b = reduce_scatter(left, hidden, 1.0, BF16)
    grad = all_gather(grad_a.astype(BF16), grad_b.astype(BF16))
    lifted, centre = lift_work(grad, hidden, probs, tile)
    centre = sum_group(centre)
    weighted0, weighted1, quad = weighted_work(lifted, centre, probs, counts)
    image_a, image_b = reduce_scatter((weighted0, weighted1), hidden, 1.0 / samples_all, BF16)
    grad_other = swap(grad, other=1)
    image = all_gather(image_a.astype(BF16), image_b.astype(BF16))
    image_other = swap(image, other=1)
    lifted2, centre2, dots = lift_work(image, hidden, probs, tile, grad)
    centre2 = sum_group(centre2)
    sums = products_work(
        samples_all, data * model, lifted, centre, lifted2, centre2, probs, counts, dots, quad
    )
    sums = lax.all_to_all(sums, ("dp", "mp"), 0, 0, tiled=True)
    size = width * local_actions * model
    return final_work(
        chips, chips, size, place, sums, (grad, grad_other), (image, image_other), tile
    )


def solution(mesh):
    placed = (
        P("dp", None),
        P(None, "mp"),
        P(None, "mp"),
        P("dp"),
        P("dp"),
        P("dp"),
        P("dp"),
        P("dp"),
        P("dp"),
        P("dp"),
    )
    return jax.shard_map(
        per_device, mesh=mesh, in_specs=placed, out_specs=P(None, "mp"), check_vma=False
    )
```

time: 572 us -> 195 us (0.34)
  waiting for transfers between devices: 341 us -> 72.7 us
  starting transfers between devices: 0.27 us -> 66 us
  matrix products: 65 us -> 0 us
  blocking collectives: 72.1 us -> 10.4 us
  Pallas kernels: 0 us -> 35.3 us
  local copies, waits for them, and re-layouts: 41.6 us -> 8.24 us
  other arithmetic: 31.6 us -> 0.98 us
  between operations: 19.2 us -> 0.36 us
    psum x3 -> x0, waiting for transfers between devices: 341 us -> none  [the longest x2 249 us: per_device(): summed = lax.psum(transpose_product(sampled, weighted), 'dp')]
    ppermute x0 -> x47, waiting for transfers between devices: none -> 72.7 us  [the longest x40 62.2 us: swap(): return lax.ppermute(x, 'dp', [(i, i ^ mask) for i in range(data)])]
    psum x7 -> x0, blocking collectives: 67.2 us -> none  [the longest x1 35.5 us: per_device(): adv_total = lax.psum(jnp.sum(advantage), 'dp')]
    ppermute x0 -> x47, starting transfers between devices: none -> 66 us  [the longest x40 55.5 us: swap(): return lax.ppermute(x, 'dp', [(i, i ^ mask) for i in range(data)])]
    dot_general x7 -> x0, matrix products: 65 us -> none  [the longest x3 34.1 us: transpose_product(): lax.dot_general(left, right, (((0,), (0,)), ((), ())), preferred_element_...]
    pallas_call x0 -> x12, Pallas kernels: none -> 35.3 us  [the longest x2 10.5 us: lift_work(): call(functools.partial(lift_kernel, dots), 'lift', grid=(width // tile,),...]
    gather x3 -> x0, local copies, waits for them, and re-layouts: 27.7 us -> none  [the longest x2 16.2 us: per_device(): sprobs = jnp.take(probs, local_rows, axis=0)]
    reduce_sum x5 -> x0, other arithmetic: 21.2 us -> none  [the longest x2 13.2 us: per_device(): curvature, = global_dots((jnp.sum(direction * fisher_image),))]
  transfers between devices with their start and end apart: 3 -> 47, of which waited for: 3 -> 26; matrix products, arithmetic and copies ran while one was open for 5% -> 1% of each run, Pallas kernels for 0% -> 10%
where the time goes in v1:
time: 195 us; the launch traced here: 194 us
  waiting for transfers between devices  72.7 us (37%)
  starting transfers between devices  66 us (34%)
  Pallas kernels  35.3 us (18%)
  blocking collectives  10.4 us (5%)
  local copies, waits for them, and re-layouts  8.24 us (4%)
    ppermute x40, waiting for transfers between devices, swap(): return lax.ppermute(x, 'dp', [(i, i ^ mask) for i in range(data)])  62.2 us
    ppermute x40, starting transfers between devices, swap(): return lax.ppermute(x, 'dp', [(i, i ^ mask) for i in range(data)])  55.5 us
    pallas_call x2, Pallas kernels, lift_work(): call(functools.partial(lift_kernel, dots), 'lift', grid=(width // tile,),...  10.5 us
    all_to_all x1, blocking collectives, per_device(): sums = lax.all_to_all(sums, ('dp', 'mp'), 0, 0, tiled=True)  10.4 us
    pallas_call x4, Pallas kernels, outer_work(): call(functools.partial(outer_kernel, pieces, scale), 'outer', grid=(colum...  10.2 us
    unnamed x30, local copies, waits for them, and re-layouts  8.12 us
    ppermute x4, starting transfers between devices, per_device(): lax.ppermute(adv_sum, 'dp', [(i, i ^ mask) for i in range(data)])  7.62 us
    pallas_call x1, Pallas kernels, final_work(): call(functools.partial(final_kernel, blocks, replicas, size), 'final', gr...  6.26 us
  transfers between devices with their start and end apart: 47, of which 26 were waited for; matrix products, arithmetic and copies ran while one was open for 1% of the time, Pallas kernels for 10%

profile of v1, /device:TPU:0, one launch (start us, length us, event | category | flops | bytes accessed | tf_op | source)
XLA Modules:
  0.0 194.1 jit_solution(4743808398024689568)
XLA Ops:
  5.0 2.9 %collective-permute-start.2 = (f32[8,128]{1,0:T(8,128)S(1)}, f32[8,128]{1,0:T(8,128)S(1)}, u32[]{:S(2)}, u32[]{:S(2)}) collective-permute-start(f32[8,128]{1,0:T(8,128)S(1)} %add.78), channel_id=1, source_target_pairs={{0,4},{2,6},{4,0},{6,2},{8,12},{10,14},{12,8},{14,10},{16,20},{18,... | collective-permute-start | bytes 12296 | tf_op jit(solution)/shard_map/ppermute | solution.py:473
  9.5 2.1 %collective-permute-start.3 = (f32[8,128]{1,0:T(8,128)S(1)}, f32[8,128]{1,0:T(8,128)S(1)}, u32[]{:S(2)}, u32[]{:S(2)}) collective-permute-start(f32[8,128]{1,0:T(8,128)S(1)} %add.79), channel_id=1, source_target_pairs={{0,8},{2,10},{4,12},{6,14},{8,0},{10,2},{12,4},{14,6},{16,24},{18,... | collective-permute-start | bytes 12296 | tf_op jit(solution)/shard_map/ppermute | solution.py:473
  14.7 6.2 %logits.1 = (f32[512,512]{1,0:T(8,128)S(1)}, f32[8,512]{1,0:T(8,128)S(1)}) custom-call(bf16[512,2560]{1,0:T(8,128)(2,1)S(1)} %copy-done, bf16[2560,512]{1,0:T(8,128)(2,1)} %w_ref.1, f32[8,512]{1,0:T(8,128)S(1)} %copy-done.4, s32[1,512]{1,0:T(1,128)S(1)} %bitcast.48), custom_call_target="tpu_custom_call" | custom-call | tf_op jit(solution)/shard_map/logits/pallas_call | solution.py:125
  23.4 2.6 %collective-permute-start.4 = (f32[8,128]{1,0:T(8,128)S(1)}, f32[8,128]{1,0:T(8,128)S(1)}, u32[]{:S(2)}, u32[]{:S(2)}) collective-permute-start(f32[8,128]{1,0:T(8,128)S(1)} %add.80), channel_id=1, source_target_pairs={{0,16},{2,18},{4,20},{6,22},{8,24},{10,26},{12,28},{14,30},{16,0},... | collective-permute-start | bytes 12296 | tf_op jit(solution)/shard_map/ppermute | solution.py:473
  34.1 2.6 %collective-permute-start.16 = (bf16[64,1024]{1,0:T(8,128)(2,1)S(1)}, bf16[64,1024]{1,0:T(8,128)(2,1)S(1)}, u32[]{:S(2)}, u32[]{:S(2)}) collective-permute-start(bf16[64,1024]{1,0:T(8,128)(2,1)S(1)} %get-tuple-element.44), channel_id=1, source_target_pairs={{0,16},{2,18},{4,20},{6,22},{8,24},{10,26},{12,28},{14,30},{16,0},... | collective-permute-start | bytes 393224 | tf_op jit(solution)/shard_map/ppermute | solution.py:420
  38.1 3.1 %outer.4 = (f32[128,1536]{1,0:T(8,128)S(1)}, bf16[128,1536]{1,0:T(8,128)(2,1)S(1)}) custom-call(bf16[256,512]{1,0:T(8,128)(2,1)S(1)} %get-tuple-element.38.left0, bf16[256,512]{1,0:T(8,128)(2,1)S(1)} %collective-permute-done.5.left1, bf16[512,2560]{1,0:T(8,128)(2,1)S(1)} %copy-done.1, bf16[512,2560]{1,0:T(8,128)(2,1)} %collective-permute-done.6.h1.refs_2_), custom_call_target="tpu_custom_call" | custom-call | tf_op jit(solution)/shard_map/outer/pallas_call | solution.py:215
  42.8 4.2 %collective-permute-done.17 = bf16[64,1024]{1,0:T(8,128)(2,1)S(1)} collective-permute-done((bf16[64,1024]{1,0:T(8,128)(2,1)S(1)}, bf16[64,1024]{1,0:T(8,128)(2,1)S(1)}, u32[]{:S(2)}, u32[]{:S(2)}) %collective-permute-start.17) | collective-permute-done | bytes 131104 | tf_op jit(solution)/shard_map/ppermute | solution.py:420
  48.7 4.3 %collective-permute-done.18 = bf16[32,1024]{1,0:T(8,128)(2,1)S(1)} collective-permute-done((bf16[32,1024]{1,0:T(8,128)(2,1)S(1)}, bf16[32,1024]{1,0:T(8,128)(2,1)S(1)}, u32[]{:S(2)}, u32[]{:S(2)}) %collective-permute-start.18) | collective-permute-done | bytes 65568 | tf_op jit(solution)/shard_map/ppermute | solution.py:420
  55.7 3.4 %collective-permute-start.10 = (bf16[32,1536]{1,0:T(8,128)(2,1)S(1)}, bf16[32,1536]{1,0:T(8,128)(2,1)S(1)}, u32[]{:S(2)}, u32[]{:S(2)}) collective-permute-start(bf16[32,1536]{1,0:T(8,128)(2,1)S(1)} %get-tuple-element.75), channel_id=1, source_target_pairs={{0,24},{2,26},{4,28},{6,30},{8,16},{10,18},{12,20},{14,22},{16,8},... | collective-permute-start | bytes 294920 | tf_op jit(solution)/shard_map/ppermute | solution.py:420
  60.8 2.6 %collective-permute-start.21 = (bf16[64,1024]{1,0:T(8,128)(2,1)S(1)}, bf16[64,1024]{1,0:T(8,128)(2,1)S(1)}, u32[]{:S(2)}, u32[]{:S(2)}) collective-permute-start(bf16[64,1024]{1,0:T(8,128)(2,1)S(1)} %pad_maximum_fusion.6), channel_id=1, source_target_pairs={{0,16},{2,18},{4,20},{6,22},{8,24},{10,26},{12,28},{14,30},{16,0},... | collective-permute-start | bytes 393224 | tf_op jit(solution)/shard_map/ppermute | solution.py:420
  64.9 5.1 %collective-permute-start.20 = (bf16[64,1024]{1,0:T(8,128)(2,1)S(1)}, bf16[64,1024]{1,0:T(8,128)(2,1)S(1)}, u32[]{:S(2)}, u32[]{:S(2)}) collective-permute-start(bf16[64,1024]{1,0:T(8,128)(2,1)S(1)} %pad_maximum_fusion.6), channel_id=1, source_target_pairs={{0,8},{2,10},{4,12},{6,14},{8,0},{10,2},{12,4},{14,6},{16,24},{18,... | collective-permute-start | bytes 393224 | tf_op jit(solution)/shard_map/ppermute | solution.py:420
  70.0 2.9 %collective-permute-done.9 = bf16[32,1536]{1,0:T(8,128)(2,1)S(1)} collective-permute-done((bf16[32,1536]{1,0:T(8,128)(2,1)S(1)}, bf16[32,1536]{1,0:T(8,128)(2,1)S(1)}, u32[]{:S(2)}, u32[]{:S(2)}) %collective-permute-start.9) | collective-permute-done | bytes 98336 | tf_op jit(solution)/shard_map/ppermute | solution.py:420
  72.9 4.2 %collective-permute-start.13 = (bf16[32,1536]{1,0:T(8,128)(2,1)S(1)}, bf16[32,1536]{1,0:T(8,128)(2,1)S(1)}, u32[]{:S(2)}, u32[]{:S(2)}) collective-permute-start(bf16[32,1536]{1,0:T(8,128)(2,1)S(1)} %get-tuple-element.68), channel_id=1, source_target_pairs={{0,24},{2,26},{4,28},{6,30},{8,16},{10,18},{12,20},{14,22},{16,8},... | collective-permute-start | bytes 294920 | tf_op jit(solution)/shard_map/ppermute | solution.py:420
  77.1 2.7 %collective-permute-start.12 = (bf16[32,1536]{1,0:T(8,128)(2,1)S(1)}, bf16[32,1536]{1,0:T(8,128)(2,1)S(1)}, u32[]{:S(2)}, u32[]{:S(2)}) collective-permute-start(bf16[32,1536]{1,0:T(8,128)(2,1)S(1)} %get-tuple-element.68), channel_id=1, source_target_pairs={{0,16},{2,18},{4,20},{6,22},{8,24},{10,26},{12,28},{14,30},{16,0},... | collective-permute-start | bytes 294920 | tf_op jit(solution)/shard_map/ppermute | solution.py:420
  81.9 4.1 %collective-permute-done.12 = bf16[32,1536]{1,0:T(8,128)(2,1)S(1)} collective-permute-done((bf16[32,1536]{1,0:T(8,128)(2,1)S(1)}, bf16[32,1536]{1,0:T(8,128)(2,1)S(1)}, u32[]{:S(2)}, u32[]{:S(2)}) %collective-permute-start.12) | collective-permute-done | bytes 98336 | tf_op jit(solution)/shard_map/ppermute | solution.py:420
  87.6 8.6 %collective-permute-done.14 = bf16[128,1536]{1,0:T(8,128)(2,1)S(1)} collective-permute-done((bf16[128,1536]{1,0:T(8,128)(2,1)S(1)}, bf16[128,1536]{1,0:T(8,128)(2,1)S(1)}, u32[]{:S(2)}, u32[]{:S(2)}) %collective-permute-start.14) | collective-permute-done | bytes 393248 | tf_op jit(solution)/shard_map/ppermute | solution.py:420
  96.3 5.0 %lift.2 = (f32[256,1024]{1,0:T(8,128)S(1)}, f32[1,1024]{1,0:T(1,128)S(1)}) custom-call(bf16[256,2560]{1,0:T(8,128)(2,1)S(1)} %pad_maximum_fusion.refs_0_.refs_5_.g0, bf16[512,2560]{1,0:T(8,128)(2,1)S(1)} %copy-done.1, bf16[512,2560]{1,0:T(8,128)(2,1)} %collective-permute-done.6.h1.refs_2_, f32[256,512]{1,0:T(8,128)S(1)} %get-tuple-element.46.refs_3_.p0, ...), custom_call_target="tpu_custom_call" | custom-call | tf_op jit(solution)/shard_map/lift/pallas_call | solution.py:267
  103.2 3.1 %collective-permute-done.25 = f32[1,1024]{1,0:T(1,128)S(1)} collective-permute-done((f32[1,1024]{1,0:T(1,128)S(1)}, f32[1,1024]{1,0:T(1,128)S(1)}, u32[]{:S(2)}, u32[]{:S(2)}) %collective-permute-start.25) | collective-permute-done | bytes 4128 | tf_op jit(solution)/shard_map/ppermute | solution.py:423
  106.6 2.0 %outer.7 = (f32[64,1024]{1,0:T(8,128)S(1)}, bf16[64,1024]{1,0:T(8,128)(2,1)S(1)}, bf16[64,1024]{1,0:T(8,128)(2,1)S(1)}, bf16[64,1024]{1,0:T(8,128)(2,1)S(1)}) custom-call(bf16[256,512]{1,0:T(8,128)(2,1)S(1)} %get-tuple-element.51.left0, bf16[256,512]{1,0:T(8,128)(2,1)S(1)} %get-tuple-element.52.left1, bf16[512,2560]{1,0:T(8,128)(2,1)S(1)} %copy-done.1, ...), custom_call_target="tpu_custom_call" | custom-call | tf_op jit(solution)/shard_map/outer/pallas_call | solution.py:215
  110.3 2.8 %collective-permute-start.37 = (bf16[64,1024]{1,0:T(8,128)(2,1)S(1)}, bf16[64,1024]{1,0:T(8,128)(2,1)S(1)}, u32[]{:S(2)}, u32[]{:S(2)}) collective-permute-start(bf16[64,1024]{1,0:T(8,128)(2,1)S(1)} %get-tuple-element.58), channel_id=1, source_target_pairs={{0,24},{2,26},{4,28},{6,30},{8,16},{10,18},{12,20},{14,22},{16,8},... | collective-permute-start | bytes 393224 | tf_op jit(solution)/shard_map/ppermute | solution.py:420
  113.1 3.1 %outer.6 = (f32[128,1536]{1,0:T(8,128)S(1)}, bf16[128,1536]{1,0:T(8,128)(2,1)S(1)}) custom-call(bf16[256,512]{1,0:T(8,128)(2,1)S(1)} %get-tuple-element.51.left0, bf16[256,512]{1,0:T(8,128)(2,1)S(1)} %get-tuple-element.52.left1, bf16[512,2560]{1,0:T(8,128)(2,1)S(1)} %copy-done.1, bf16[512,2560]{1,0:T(8,128)(2,1)} %collective-permute-done.6.h1.refs_2_), custom_call_target="tpu_custom_call" | custom-call | tf_op jit(solution)/shard_map/outer/pallas_call | solution.py:215
  116.7 4.4 %collective-permute-done.36 = bf16[64,1024]{1,0:T(8,128)(2,1)S(1)} collective-permute-done((bf16[64,1024]{1,0:T(8,128)(2,1)S(1)}, bf16[64,1024]{1,0:T(8,128)(2,1)S(1)}, u32[]{:S(2)}, u32[]{:S(2)}) %collective-permute-start.36) | collective-permute-done | bytes 131104 | tf_op jit(solution)/shard_map/ppermute | solution.py:420
  121.8 5.0 %collective-permute-done.38 = bf16[32,1024]{1,0:T(8,128)(2,1)S(1)} collective-permute-done((bf16[32,1024]{1,0:T(8,128)(2,1)S(1)}, bf16[32,1024]{1,0:T(8,128)(2,1)S(1)}, u32[]{:S(2)}, u32[]{:S(2)}) %collective-permute-start.38) | collective-permute-done | bytes 65568 | tf_op jit(solution)/shard_map/ppermute | solution.py:420
  135.9 7.4 %collective-permute-start.40 = (bf16[64,1024]{1,0:T(8,128)(2,1)S(1)}, bf16[64,1024]{1,0:T(8,128)(2,1)S(1)}, u32[]{:S(2)}, u32[]{:S(2)}) collective-permute-start(bf16[64,1024]{1,0:T(8,128)(2,1)S(1)} %pad_maximum_fusion.7), channel_id=1, source_target_pairs={{0,8},{2,10},{4,12},{6,14},{8,0},{10,2},{12,4},{14,6},{16,24},{18,... | collective-permute-start | bytes 393224 | tf_op jit(solution)/shard_map/ppermute | solution.py:420
  143.3 2.7 %collective-permute-done.29 = bf16[32,1536]{1,0:T(8,128)(2,1)S(1)} collective-permute-done((bf16[32,1536]{1,0:T(8,128)(2,1)S(1)}, bf16[32,1536]{1,0:T(8,128)(2,1)S(1)}, u32[]{:S(2)}, u32[]{:S(2)}) %collective-permute-start.29) | collective-permute-done | bytes 98336 | tf_op jit(solution)/shard_map/ppermute | solution.py:420
  148.6 5.2 %collective-permute-done.41 = bf16[64,1024]{1,0:T(8,128)(2,1)S(1)} collective-permute-done((bf16[64,1024]{1,0:T(8,128)(2,1)S(1)}, bf16[64,1024]{1,0:T(8,128)(2,1)S(1)}, u32[]{:S(2)}, u32[]{:S(2)}) %collective-permute-start.41) | collective-permute-done | bytes 131104 | tf_op jit(solution)/shard_map/ppermute | solution.py:420
  153.8 3.3 %collective-permute-done.32 = bf16[32,1536]{1,0:T(8,128)(2,1)S(1)} collective-permute-done((bf16[32,1536]{1,0:T(8,128)(2,1)S(1)}, bf16[32,1536]{1,0:T(8,128)(2,1)S(1)}, u32[]{:S(2)}, u32[]{:S(2)}) %collective-permute-start.32) | collective-permute-done | bytes 98336 | tf_op jit(solution)/shard_map/ppermute | solution.py:420
  160.0 6.2 %collective-permute-done.34 = bf16[128,1536]{1,0:T(8,128)(2,1)S(1)} collective-permute-done((bf16[128,1536]{1,0:T(8,128)(2,1)S(1)}, bf16[128,1536]{1,0:T(8,128)(2,1)S(1)}, u32[]{:S(2)}, u32[]{:S(2)}) %collective-permute-start.34) | collective-permute-done | bytes 393248 | tf_op jit(solution)/shard_map/ppermute | solution.py:420
  166.5 5.5 %lift.3 = (f32[256,1024]{1,0:T(8,128)S(1)}, f32[1,1024]{1,0:T(1,128)S(1)}, f32[8,128]{1,0:T(8,128)S(1)}) custom-call(bf16[256,2560]{1,0:T(8,128)(2,1)S(1)} %pad_maximum_fusion.1.refs_0_.f0, bf16[512,2560]{1,0:T(8,128)(2,1)} %refs_1_.3, bf16[512,2560]{1,0:T(8,128)(2,1)} %collective-permute-done.6.h1.refs_2_, f32[256,512]{1,0:T(8,128)S(1)} %get-tuple-element.46.refs_3_.p0, ...), custom_call_target="tpu_custom_call" | custom-call | tf_op jit(solution)/shard_map/lift/pallas_call | solution.py:267
  174.1 2.9 %collective-permute-done.44 = f32[1,1024]{1,0:T(1,128)S(1)} collective-permute-done((f32[1,1024]{1,0:T(1,128)S(1)}, f32[1,1024]{1,0:T(1,128)S(1)}, u32[]{:S(2)}, u32[]{:S(2)}) %collective-permute-start.44) | collective-permute-done | bytes 4128 | tf_op jit(solution)/shard_map/ppermute | solution.py:423
  177.4 10.4 %all_to_all.11 = f32[32,1,128]{2,1,0:T(1,128)S(1)} all-to-all(f32[32,1,128]{2,1,0:T(1,128)S(1)} %bitcast.46), channel_id=1, replica_groups=mesh['dp'=16,'mp'=2] {'dp','mp'}, dimensions={0} | all-to-all | bytes 32768 | tf_op jit(solution)/shard_map/all_to_all | solution.py:498
  187.8 6.3 %final.1 = f32[2560,512]{1,0:T(8,128)} custom-call(s32[3]{0:T(128)S(1)} %pad_add_fusion.place_ref, f32[32,128]{1,0:T(8,128)S(1)} %bitcast.45, bf16[256,2560]{1,0:T(8,128)(2,1)S(1)} %pad_maximum_fusion.refs_0_.refs_5_.g0, bf16[256,2560]{1,0:T(8,128)(2,1)S(1)} %collective-permute-done.45.g1, bf16[256,2560]{1,0:T(8,128)(2,1)S(1)} %pad_maximum_fusion.1.refs_0_.f0, ...), custom_call_target="tpu_custom_call" | custom-call | tf_op jit(solution)/shard_map/final/pallas_call | solution.py:373
  (138 shorter events, 57.0 us)
Async XLA Ops:
  0.0 31.6 %collective-permute-start.6 = (bf16[512,2560]{1,0:T(8,128)(2,1)}, bf16[512,2560]{1,0:T(8,128)(2,1)}, u32[]{:S(2)}, u32[]{:S(2)}) collective-permute-start(bf16[512,2560]{1,0:T(8,128)(2,1)} %refs_1_.3), channel_id=1, source_target_pairs={{0,2},{2,0},{4,6},{6,4},{8,10},{10,8},{12,14},{14,12},{16,18},{18,... | collective-permute-start | bytes 7864328 | tf_op jit(solution)/shard_map/ppermute | solution.py:420
  9.5 13.9 %collective-permute-start.3 = (f32[8,128]{1,0:T(8,128)S(1)}, f32[8,128]{1,0:T(8,128)S(1)}, u32[]{:S(2)}, u32[]{:S(2)}) collective-permute-start(f32[8,128]{1,0:T(8,128)S(1)} %add.79), channel_id=1, source_target_pairs={{0,8},{2,10},{4,12},{6,14},{8,0},{10,2},{12,4},{14,6},{16,24},{18,... | collective-permute-start | bytes 12296 | tf_op jit(solution)/shard_map/ppermute | solution.py:473
  21.9 6.0 %collective-permute-start = (f32[8,512]{1,0:T(8,128)S(1)}, f32[8,512]{1,0:T(8,128)S(1)}, u32[]{:S(2)}, u32[]{:S(2)}) collective-permute-start(f32[8,512]{1,0:T(8,128)S(1)} %get-tuple-element.35.stats_ref), channel_id=1, source_target_pairs={{0,1},{1,0},{2,3},{3,2},{4,5},{5,4},{6,7},{7,6},{8,9},{9,8},{10,11... | collective-permute-start | bytes 49160 | tf_op jit(solution)/shard_map/ppermute | solution.py:423
  33.6 9.1 %collective-permute-start.15 = (bf16[64,1024]{1,0:T(8,128)(2,1)S(1)}, bf16[64,1024]{1,0:T(8,128)(2,1)S(1)}, u32[]{:S(2)}, u32[]{:S(2)}) collective-permute-start(bf16[64,1024]{1,0:T(8,128)(2,1)S(1)} %get-tuple-element.43), channel_id=1, source_target_pairs={{0,8},{2,10},{4,12},{6,14},{8,0},{10,2},{12,4},{14,6},{16,24},{18,... | collective-permute-start | bytes 393224 | tf_op jit(solution)/shard_map/ppermute | solution.py:420
  34.1 8.6 %collective-permute-start.16 = (bf16[64,1024]{1,0:T(8,128)(2,1)S(1)}, bf16[64,1024]{1,0:T(8,128)(2,1)S(1)}, u32[]{:S(2)}, u32[]{:S(2)}) collective-permute-start(bf16[64,1024]{1,0:T(8,128)(2,1)S(1)} %get-tuple-element.44), channel_id=1, source_target_pairs={{0,16},{2,18},{4,20},{6,22},{8,24},{10,26},{12,28},{14,30},{16,0},... | collective-permute-start | bytes 393224 | tf_op jit(solution)/shard_map/ppermute | solution.py:420
  36.7 10.3 %collective-permute-start.17 = (bf16[64,1024]{1,0:T(8,128)(2,1)S(1)}, bf16[64,1024]{1,0:T(8,128)(2,1)S(1)}, u32[]{:S(2)}, u32[]{:S(2)}) collective-permute-start(bf16[64,1024]{1,0:T(8,128)(2,1)S(1)} %get-tuple-element.45), channel_id=1, source_target_pairs={{0,24},{2,26},{4,28},{6,30},{8,16},{10,18},{12,20},{14,22},{16,8},... | collective-permute-start | bytes 393224 | tf_op jit(solution)/shard_map/ppermute | solution.py:420
  41.2 13.4 %collective-permute-start.7 = (bf16[128,1536]{1,0:T(8,128)(2,1)S(1)}, bf16[128,1536]{1,0:T(8,128)(2,1)S(1)}, u32[]{:S(2)}, u32[]{:S(2)}) collective-permute-start(bf16[128,1536]{1,0:T(8,128)(2,1)S(1)} %get-tuple-element.41), channel_id=1, source_target_pairs={{0,4},{2,6},{4,0},{6,2},{8,12},{10,14},{12,8},{14,10},{16,20},{18,... | collective-permute-start | bytes 1179656 | tf_op jit(solution)/shard_map/ppermute | solution.py:420
  48.6 47.6 %collective-permute-start.23 = (f32[256,512]{1,0:T(8,128)S(1)}, f32[256,512]{1,0:T(8,128)S(1)}, u32[]{:S(2)}, u32[]{:S(2)}) collective-permute-start(f32[256,512]{1,0:T(8,128)S(1)} %get-tuple-element.47), channel_id=1, source_target_pairs={{0,2},{2,0},{4,6},{6,4},{8,10},{10,8},{12,14},{14,12},{16,18},{18,... | collective-permute-start | bytes 1572872 | tf_op jit(solution)/shard_map/ppermute | solution.py:420
  53.0 6.1 %collective-permute-start.19 = (bf16[32,1024]{1,0:T(8,128)(2,1)S(1)}, bf16[32,1024]{1,0:T(8,128)(2,1)S(1)}, u32[]{:S(2)}, u32[]{:S(2)}) collective-permute-start(bf16[32,1024]{1,0:T(8,128)(2,1)S(1)} %fusion.7), channel_id=1, source_target_pairs={{0,4},{2,6},{4,0},{6,2},{8,12},{10,14},{12,8},{14,10},{16,20},{18,... | collective-permute-start | bytes 196616 | tf_op jit(solution)/shard_map/ppermute | solution.py:420
  54.7 6.1 %collective-permute-start.8 = (bf16[32,1536]{1,0:T(8,128)(2,1)S(1)}, bf16[32,1536]{1,0:T(8,128)(2,1)S(1)}, u32[]{:S(2)}, u32[]{:S(2)}) collective-permute-start(bf16[32,1536]{1,0:T(8,128)(2,1)S(1)} %get-tuple-element.74), channel_id=1, source_target_pairs={{0,8},{2,10},{4,12},{6,14},{8,0},{10,2},{12,4},{14,6},{16,24},{18,... | collective-permute-start | bytes 294920 | tf_op jit(solution)/shard_map/ppermute | solution.py:420
  55.7 9.2 %collective-permute-start.10 = (bf16[32,1536]{1,0:T(8,128)(2,1)S(1)}, bf16[32,1536]{1,0:T(8,128)(2,1)S(1)}, u32[]{:S(2)}, u32[]{:S(2)}) collective-permute-start(bf16[32,1536]{1,0:T(8,128)(2,1)S(1)} %get-tuple-element.75), channel_id=1, source_target_pairs={{0,24},{2,26},{4,28},{6,30},{8,16},{10,18},{12,20},{14,22},{16,8},... | collective-permute-start | bytes 294920 | tf_op jit(solution)/shard_map/ppermute | solution.py:420
  59.1 13.8 %collective-permute-start.9 = (bf16[32,1536]{1,0:T(8,128)(2,1)S(1)}, bf16[32,1536]{1,0:T(8,128)(2,1)S(1)}, u32[]{:S(2)}, u32[]{:S(2)}) collective-permute-start(bf16[32,1536]{1,0:T(8,128)(2,1)S(1)} %get-tuple-element.76), channel_id=1, source_target_pairs={{0,16},{2,18},{4,20},{6,22},{8,24},{10,26},{12,28},{14,30},{16,0},... | collective-permute-start | bytes 294920 | tf_op jit(solution)/shard_map/ppermute | solution.py:420
  59.1 18.0 %collective-permute-start.22 = (bf16[64,1024]{1,0:T(8,128)(2,1)S(1)}, bf16[64,1024]{1,0:T(8,128)(2,1)S(1)}, u32[]{:S(2)}, u32[]{:S(2)}) collective-permute-start(bf16[64,1024]{1,0:T(8,128)(2,1)S(1)} %pad_maximum_fusion.6), channel_id=1, source_target_pairs={{0,24},{2,26},{4,28},{6,30},{8,16},{10,18},{12,20},{14,22},{16,8},... | collective-permute-start | bytes 393224 | tf_op jit(solution)/shard_map/ppermute | solution.py:420
  60.8 20.8 %collective-permute-start.21 = (bf16[64,1024]{1,0:T(8,128)(2,1)S(1)}, bf16[64,1024]{1,0:T(8,128)(2,1)S(1)}, u32[]{:S(2)}, u32[]{:S(2)}) collective-permute-start(bf16[64,1024]{1,0:T(8,128)(2,1)S(1)} %pad_maximum_fusion.6), channel_id=1, source_target_pairs={{0,16},{2,18},{4,20},{6,22},{8,24},{10,26},{12,28},{14,30},{16,0},... | collective-permute-start | bytes 393224 | tf_op jit(solution)/shard_map/ppermute | solution.py:420
  64.9 16.9 %collective-permute-start.20 = (bf16[64,1024]{1,0:T(8,128)(2,1)S(1)}, bf16[64,1024]{1,0:T(8,128)(2,1)S(1)}, u32[]{:S(2)}, u32[]{:S(2)}) collective-permute-start(bf16[64,1024]{1,0:T(8,128)(2,1)S(1)} %pad_maximum_fusion.6), channel_id=1, source_target_pairs={{0,8},{2,10},{4,12},{6,14},{8,0},{10,2},{12,4},{14,6},{16,24},{18,... | collective-permute-start | bytes 393224 | tf_op jit(solution)/shard_map/ppermute | solution.py:420
  72.9 9.0 %collective-permute-start.13 = (bf16[32,1536]{1,0:T(8,128)(2,1)S(1)}, bf16[32,1536]{1,0:T(8,128)(2,1)S(1)}, u32[]{:S(2)}, u32[]{:S(2)}) collective-permute-start(bf16[32,1536]{1,0:T(8,128)(2,1)S(1)} %get-tuple-element.68), channel_id=1, source_target_pairs={{0,24},{2,26},{4,28},{6,30},{8,16},{10,18},{12,20},{14,22},{16,8},... | collective-permute-start | bytes 294920 | tf_op jit(solution)/shard_map/ppermute | solution.py:420
  77.1 8.9 %collective-permute-start.12 = (bf16[32,1536]{1,0:T(8,128)(2,1)S(1)}, bf16[32,1536]{1,0:T(8,128)(2,1)S(1)}, u32[]{:S(2)}, u32[]{:S(2)}) collective-permute-start(bf16[32,1536]{1,0:T(8,128)(2,1)S(1)} %get-tuple-element.68), channel_id=1, source_target_pairs={{0,16},{2,18},{4,20},{6,22},{8,24},{10,26},{12,28},{14,30},{16,0},... | collective-permute-start | bytes 294920 | tf_op jit(solution)/shard_map/ppermute | solution.py:420
  87.0 9.2 %collective-permute-start.14 = (bf16[128,1536]{1,0:T(8,128)(2,1)S(1)}, bf16[128,1536]{1,0:T(8,128)(2,1)S(1)}, u32[]{:S(2)}, u32[]{:S(2)}) collective-permute-start(bf16[128,1536]{1,0:T(8,128)(2,1)S(1)} %pad_maximum_fusion.4), channel_id=1, source_target_pairs={{0,4},{2,6},{4,0},{6,2},{8,12},{10,14},{12,8},{14,10},{16,20},{18,... | collective-permute-start | bytes 1179656 | tf_op jit(solution)/shard_map/ppermute | solution.py:420
  108.6 8.1 %collective-permute-start.35 = (bf16[64,1024]{1,0:T(8,128)(2,1)S(1)}, bf16[64,1024]{1,0:T(8,128)(2,1)S(1)}, u32[]{:S(2)}, u32[]{:S(2)}) collective-permute-start(bf16[64,1024]{1,0:T(8,128)(2,1)S(1)} %get-tuple-element.56), channel_id=1, source_target_pairs={{0,8},{2,10},{4,12},{6,14},{8,0},{10,2},{12,4},{14,6},{16,24},{18,... | collective-permute-start | bytes 393224 | tf_op jit(solution)/shard_map/ppermute | solution.py:420
  108.7 12.5 %collective-permute-start.36 = (bf16[64,1024]{1,0:T(8,128)(2,1)S(1)}, bf16[64,1024]{1,0:T(8,128)(2,1)S(1)}, u32[]{:S(2)}, u32[]{:S(2)}) collective-permute-start(bf16[64,1024]{1,0:T(8,128)(2,1)S(1)} %get-tuple-element.57), channel_id=1, source_target_pairs={{0,16},{2,18},{4,20},{6,22},{8,24},{10,26},{12,28},{14,30},{16,0},... | collective-permute-start | bytes 393224 | tf_op jit(solution)/shard_map/ppermute | solution.py:420
  110.3 10.8 %collective-permute-start.37 = (bf16[64,1024]{1,0:T(8,128)(2,1)S(1)}, bf16[64,1024]{1,0:T(8,128)(2,1)S(1)}, u32[]{:S(2)}, u32[]{:S(2)}) collective-permute-start(bf16[64,1024]{1,0:T(8,128)(2,1)S(1)} %get-tuple-element.58), channel_id=1, source_target_pairs={{0,24},{2,26},{4,28},{6,30},{8,16},{10,18},{12,20},{14,22},{16,8},... | collective-permute-start | bytes 393224 | tf_op jit(solution)/shard_map/ppermute | solution.py:420
  116.2 11.3 %collective-permute-start.27 = (bf16[128,1536]{1,0:T(8,128)(2,1)S(1)}, bf16[128,1536]{1,0:T(8,128)(2,1)S(1)}, u32[]{:S(2)}, u32[]{:S(2)}) collective-permute-start(bf16[128,1536]{1,0:T(8,128)(2,1)S(1)} %get-tuple-element.54), channel_id=1, source_target_pairs={{0,4},{2,6},{4,0},{6,2},{8,12},{10,14},{12,8},{14,10},{16,20},{18,... | collective-permute-start | bytes 1179656 | tf_op jit(solution)/shard_map/ppermute | solution.py:420
  121.8 66.0 %collective-permute-start.45 = (bf16[256,2560]{1,0:T(8,128)(2,1)S(1)}, bf16[256,2560]{1,0:T(8,128)(2,1)S(1)}, u32[]{:S(2)}, u32[]{:S(2)}) collective-permute-start(bf16[256,2560]{1,0:T(8,128)(2,1)S(1)} %pad_maximum_fusion.refs_0_.refs_5_.g0), channel_id=1, source_target_pairs={{0,2},{2,0},{4,6},{6,4},{8,10},{10,8},{12,14},{14,12},{16,18},{18,... | collective-permute-start | bytes 3932168 | tf_op jit(solution)/shard_map/ppermute | solution.py:420
  128.3 7.6 %collective-permute-start.30 = (bf16[32,1536]{1,0:T(8,128)(2,1)S(1)}, bf16[32,1536]{1,0:T(8,128)(2,1)S(1)}, u32[]{:S(2)}, u32[]{:S(2)}) collective-permute-start(bf16[32,1536]{1,0:T(8,128)(2,1)S(1)} %get-tuple-element.72), channel_id=1, source_target_pairs={{0,24},{2,26},{4,28},{6,30},{8,16},{10,18},{12,20},{14,22},{16,8},... | collective-permute-start | bytes 294920 | tf_op jit(solution)/shard_map/ppermute | solution.py:420
  129.7 16.3 %collective-permute-start.29 = (bf16[32,1536]{1,0:T(8,128)(2,1)S(1)}, bf16[32,1536]{1,0:T(8,128)(2,1)S(1)}, u32[]{:S(2)}, u32[]{:S(2)}) collective-permute-start(bf16[32,1536]{1,0:T(8,128)(2,1)S(1)} %get-tuple-element.73), channel_id=1, source_target_pairs={{0,16},{2,18},{4,20},{6,22},{8,24},{10,26},{12,28},{14,30},{16,0},... | collective-permute-start | bytes 294920 | tf_op jit(solution)/shard_map/ppermute | solution.py:420
  131.2 15.6 %collective-permute-start.42 = (bf16[64,1024]{1,0:T(8,128)(2,1)S(1)}, bf16[64,1024]{1,0:T(8,128)(2,1)S(1)}, u32[]{:S(2)}, u32[]{:S(2)}) collective-permute-start(bf16[64,1024]{1,0:T(8,128)(2,1)S(1)} %pad_maximum_fusion.7), channel_id=1, source_target_pairs={{0,24},{2,26},{4,28},{6,30},{8,16},{10,18},{12,20},{14,22},{16,8},... | collective-permute-start | bytes 393224 | tf_op jit(solution)/shard_map/ppermute | solution.py:420
  133.0 20.8 %collective-permute-start.41 = (bf16[64,1024]{1,0:T(8,128)(2,1)S(1)}, bf16[64,1024]{1,0:T(8,128)(2,1)S(1)}, u32[]{:S(2)}, u32[]{:S(2)}) collective-permute-start(bf16[64,1024]{1,0:T(8,128)(2,1)S(1)} %pad_maximum_fusion.7), channel_id=1, source_target_pairs={{0,16},{2,18},{4,20},{6,22},{8,24},{10,26},{12,28},{14,30},{16,0},... | collective-permute-start | bytes 393224 | tf_op jit(solution)/shard_map/ppermute | solution.py:420
  135.9 17.9 %collective-permute-start.40 = (bf16[64,1024]{1,0:T(8,128)(2,1)S(1)}, bf16[64,1024]{1,0:T(8,128)(2,1)S(1)}, u32[]{:S(2)}, u32[]{:S(2)}) collective-permute-start(bf16[64,1024]{1,0:T(8,128)(2,1)S(1)} %pad_maximum_fusion.7), channel_id=1, source_target_pairs={{0,8},{2,10},{4,12},{6,14},{8,0},{10,2},{12,4},{14,6},{16,24},{18,... | collective-permute-start | bytes 393224 | tf_op jit(solution)/shard_map/ppermute | solution.py:420
  146.1 7.8 %collective-permute-start.33 = (bf16[32,1536]{1,0:T(8,128)(2,1)S(1)}, bf16[32,1536]{1,0:T(8,128)(2,1)S(1)}, u32[]{:S(2)}, u32[]{:S(2)}) collective-permute-start(bf16[32,1536]{1,0:T(8,128)(2,1)S(1)} %get-tuple-element.64), channel_id=1, source_target_pairs={{0,24},{2,26},{4,28},{6,30},{8,16},{10,18},{12,20},{14,22},{16,8},... | collective-permute-start | bytes 294920 | tf_op jit(solution)/shard_map/ppermute | solution.py:420
  146.8 10.4 %collective-permute-start.32 = (bf16[32,1536]{1,0:T(8,128)(2,1)S(1)}, bf16[32,1536]{1,0:T(8,128)(2,1)S(1)}, u32[]{:S(2)}, u32[]{:S(2)}) collective-permute-start(bf16[32,1536]{1,0:T(8,128)(2,1)S(1)} %get-tuple-element.64), channel_id=1, source_target_pairs={{0,16},{2,18},{4,20},{6,22},{8,24},{10,26},{12,28},{14,30},{16,0},... | collective-permute-start | bytes 294920 | tf_op jit(solution)/shard_map/ppermute | solution.py:420
  158.4 7.8 %collective-permute-start.34 = (bf16[128,1536]{1,0:T(8,128)(2,1)S(1)}, bf16[128,1536]{1,0:T(8,128)(2,1)S(1)}, u32[]{:S(2)}, u32[]{:S(2)}) collective-permute-start(bf16[128,1536]{1,0:T(8,128)(2,1)S(1)} %pad_maximum_fusion.5), channel_id=1, source_target_pairs={{0,4},{2,6},{4,0},{6,2},{8,12},{10,14},{12,8},{14,10},{16,20},{18,... | collective-permute-start | bytes 1179656 | tf_op jit(solution)/shard_map/ppermute | solution.py:420
  166.4 21.5 %collective-permute-start.46 = (bf16[256,2560]{1,0:T(8,128)(2,1)S(1)}, bf16[256,2560]{1,0:T(8,128)(2,1)S(1)}, u32[]{:S(2)}, u32[]{:S(2)}) collective-permute-start(bf16[256,2560]{1,0:T(8,128)(2,1)S(1)} %pad_maximum_fusion.1.refs_0_.f0), channel_id=1, source_target_pairs={{0,2},{2,0},{4,6},{6,4},{8,10},{10,8},{12,14},{14,12},{16,18},{18,... | collective-permute-start | bytes 3932168 | tf_op jit(solution)/shard_map/ppermute | solution.py:420
  (27 other events, 107.4 us)
